TPU v7x, 512 devices: a whole 4x4x16 slice. The times are simulated.
512 devices in a mesh: orient: 32 (over y_lo, z), brow: 2 (over core), bcol: 8 (over x, y_hi).
Axes of the slice: x: 4, y: 4 (y_hi: 2, y_lo: 2; y = y_hi * 2 + y_lo), z: 16, core: 2. Of those that a mesh axis runs over, the one named last changes fastest.
Arguments:
- volume: float32 [32, 64, 832], P('orient', 'brow', 'bcol'), may hold values from -700 to 700
- template: float32 [24, 24, 24], replicated, may hold values from 0 to 1
- voxel_maps: int32 [32, 13824], P('orient'), may hold values from 0 to 13823, as said below
Outputs:
- best: float32 [32, 64, 832], P('orient', 'brow', 'bcol')
Inputs may be any that keep to these rules, and one draw needn't show every extreme that they name: `voxel_maps`: each row holds every number of 0 to 13823 exactly once.
All inputs are finite; a program needn't handle non-finite values.
Results may differ from a plain program's by a relative error of at most 0.00013.
Values sent between devices are 32-bit elements; how exact they have to be, the bound alone decides.
No kernel may reach another device: no remote copies, remote signals or barrier semaphores. Data moves between devices by JAX's collectives and lax.ppermute only.
A program may use at most 64 MiB of HBM per device.

v0:
```python
import math
import jax
import jax.numpy as jnp
from jax import lax
from jax.sharding import PartitionSpec as P

epsilon = 1e-06
floor_share = 0.1
highest = lax.Precision.HIGHEST


def extended(cells, sides, width):
    for axis, dim in sides:
        count = lax.axis_size(axis)
        ends = count - 1
        head = lax.slice_in_dim(cells, 0, width, axis=dim)
        tail = lax.slice_in_dim(cells, cells.shape[dim] - width, cells.shape[dim], axis=dim)
        cells = jnp.concatenate(
            [
                lax.ppermute(tail, axis, [(i, (i + 1) % count) for i in range(ends)]),
                cells,
                lax.ppermute(head, axis, [((i + 1) % count, i) for i in range(ends)]),
            ],
            axis=dim,
        )
    return cells


def phase_tables(row_index, col_index, length):
    products = row_index[:, None] * col_index[None, :] % length
    angles = products.astype(jnp.float32) * (2.0 * math.pi / length)
    return (jnp.cos(angles), jnp.sin(angles))


def band_table(row_index, col_index, lower, upper):
    offsets = col_index[None, :] - row_index[:, None]
    return ((offsets >= lower) & (offsets < upper)).astype(jnp.float32)


def whiten_rows(rows_in):
    length = rows_in.shape[-1]
    frequency = jnp.arange(length, dtype=jnp.int32)
    cosine, sine_table = phase_tables(frequency, frequency, length)
    spec_real = jnp.dot(rows_in, cosine, precision=highest)
    spec_imag = -jnp.dot(rows_in, sine_table, precision=highest)
    power_spec = spec_real * spec_real + spec_imag * spec_imag
    smoothed = (
        jnp.roll(power_spec, 1, axis=1) + power_spec + jnp.roll(power_spec, -1, axis=1)
    ) / 3.0
    smoothed = smoothed + floor_share * jnp.mean(power_spec, axis=1, keepdims=True) + epsilon
    weights = lax.rsqrt(smoothed)
    whitened = jnp.dot(spec_real * weights, cosine, precision=highest) - jnp.dot(
        spec_imag * weights, sine_table, precision=highest
    )
    return whitened / math.sqrt(length)


def shards(volume, template, voxel_maps):
    plane_count, brick_rows, brick_cols = volume.shape
    template_edge = template.shape[0]
    half_edge = template_edge // 2
    depth_total = plane_count * lax.axis_size("orient")
    pad_rows = brick_rows + template_edge
    pad_cols = brick_cols + template_edge
    pad_depth = depth_total + template_edge
    pencils = lax.all_to_all(volume, "bcol", split_axis=1, concat_axis=2, tiled=True)
    whitened_rows = whiten_rows(pencils.reshape(-1, pencils.shape[-1])).reshape(pencils.shape)
    whitened = lax.all_to_all(whitened_rows, "bcol", split_axis=2, concat_axis=1, tiled=True)
    padded = extended(whitened, (("brow", 1), ("bcol", 2)), half_edge)
    col_freq = jnp.arange(pad_cols, dtype=jnp.int32)
    row_freq = jnp.arange(pad_rows, dtype=jnp.int32)
    depth_freq = jnp.arange(pad_depth, dtype=jnp.int32)
    depth_index = jnp.arange(depth_total, dtype=jnp.int32)
    tpl_index = jnp.arange(template_edge, dtype=jnp.int32)
    out_rows = jnp.arange(brick_rows, dtype=jnp.int32)
    out_cols = jnp.arange(brick_cols, dtype=jnp.int32)
    cos_cols, sin_cols = phase_tables(col_freq, col_freq, pad_cols)
    cos_rows, sin_rows = phase_tables(row_freq, row_freq, pad_rows)
    cos_depth, sin_depth = phase_tables(depth_freq, depth_index, pad_depth)
    tcos_cols, tsin_cols = phase_tables(tpl_index, col_freq, pad_cols)
    tcos_rows, tsin_rows = phase_tables(row_freq, tpl_index, pad_rows)
    tcos_depth, tsin_depth = phase_tables(depth_freq, tpl_index, pad_depth)
    back_depth_c, back_depth_s = phase_tables(depth_index - half_edge, depth_freq, pad_depth)
    back_rows_c, back_rows_s = phase_tables(out_rows, row_freq, pad_rows)
    back_cols_c, back_cols_s = phase_tables(col_freq, out_cols, pad_cols)
    box_rows = band_table(out_rows, row_freq, 0, template_edge)
    box_cols = band_table(out_cols, col_freq, 0, template_edge).T
    box_depth = band_table(depth_index, depth_index, -half_edge, half_edge)
    portion = lax.all_gather(padded, "orient", axis=0, tiled=True)
    col_real = jnp.einsum("nxy,yk->nxk", portion, cos_cols, precision=highest)
    col_imag = -jnp.einsum("nxy,yk->nxk", portion, sin_cols, precision=highest)
    spec_real = jnp.einsum("kx,nxy->nky", cos_rows, col_real, precision=highest) + jnp.einsum(
        "kx,nxy->nky", sin_rows, col_imag, precision=highest
    )
    spec_imag = jnp.einsum("kx,nxy->nky", cos_rows, col_imag, precision=highest) - jnp.einsum(
        "kx,nxy->nky", sin_rows, col_real, precision=highest
    )
    squares = portion * portion
    along_cols = jnp.einsum("nxy,yr->nxr", squares, box_cols, precision=highest)
    sum_real = jnp.einsum("kz,zxy->kxy", cos_depth, spec_real, precision=highest) + jnp.einsum(
        "kz,zxy->kxy", sin_depth, spec_imag, precision=highest
    )
    sum_imag = jnp.einsum("kz,zxy->kxy", cos_depth, spec_imag, precision=highest) - jnp.einsum(
        "kz,zxy->kxy", sin_depth, spec_real, precision=highest
    )
    sum_energy = jnp.einsum(
        "wz,zqr->wqr",
        box_depth,
        jnp.einsum("qx,nxr->nqr", box_rows, along_cols, precision=highest),
        precision=highest,
    )
    flattened = template.reshape(-1)
    centred = flattened - jnp.mean(flattened)
    normed = centred / jnp.sqrt(jnp.sum(centred * centred) + epsilon)
    voxel_total = flattened.shape[0]
    scaling = lax.rsqrt(sum_energy / voxel_total + epsilon)
    inverse_norm = 1.0 / (pad_depth * pad_rows * pad_cols)
    rotated = normed[voxel_maps[0]].reshape(template_edge, template_edge, template_edge)
    tcol_real = jnp.einsum("abc,ck->abk", rotated, tcos_cols, precision=highest)
    tcol_imag = -jnp.einsum("abc,ck->abk", rotated, tsin_cols, precision=highest)
    trow_real = jnp.einsum("kb,abc->akc", tcos_rows, tcol_real, precision=highest) + jnp.einsum(
        "kb,abc->akc", tsin_rows, tcol_imag, precision=highest
    )
    trow_imag = jnp.einsum("kb,abc->akc", tcos_rows, tcol_imag, precision=highest) - jnp.einsum(
        "kb,abc->akc", tsin_rows, tcol_real, precision=highest
    )
    tpl_real = jnp.einsum("ka,abc->kbc", tcos_depth, trow_real, precision=highest) + jnp.einsum(
        "ka,abc->kbc", tsin_depth, trow_imag, precision=highest
    )
    tpl_imag = jnp.einsum("ka,abc->kbc", tcos_depth, trow_imag, precision=highest) - jnp.einsum(
        "ka,abc->kbc", tsin_depth, trow_real, precision=highest
    )
    prod_real = sum_real * tpl_real + sum_imag * tpl_imag
    prod_imag = sum_imag * tpl_real - sum_real * tpl_imag
    depth_real = jnp.einsum("zk,kxy->zxy", back_depth_c, prod_real, precision=highest) - jnp.einsum(
        "zk,kxy->zxy", back_depth_s, prod_imag, precision=highest
    )
    depth_imag = jnp.einsum("zk,kxy->zxy", back_depth_c, prod_imag, precision=highest) + jnp.einsum(
        "zk,kxy->zxy", back_depth_s, prod_real, precision=highest
    )
    rows_real = jnp.einsum("qk,zky->zqy", back_rows_c, depth_real, precision=highest) - jnp.einsum(
        "qk,zky->zqy", back_rows_s, depth_imag, precision=highest
    )
    rows_imag = jnp.einsum("qk,zky->zqy", back_rows_c, depth_imag, precision=highest) + jnp.einsum(
        "qk,zky->zqy", back_rows_s, depth_real, precision=highest
    )
    correlation = jnp.einsum("zqk,kr->zqr", rows_real, back_cols_c, precision=highest) - jnp.einsum(
        "zqk,kr->zqr", rows_imag, back_cols_s, precision=highest
    )
    score = correlation * inverse_norm * scaling
    combined = lax.pmax(score, "orient")
    return lax.dynamic_slice_in_dim(
        combined, lax.axis_index("orient") * plane_count, plane_count, 0
    )


def solution(mesh):
    in_specs = (P("orient", "brow", "bcol"), P(), P("orient", None))
    out_specs = P("orient", "brow", "bcol")
    return jax.shard_map(shards, mesh=mesh, in_specs=in_specs, out_specs=out_specs, check_vma=False)
```

profile of v0, /device:TPU:2, one launch (start us, length us, event | category | flops | bytes accessed | tf_op | source)
XLA Modules:
  0.0 549.8 jit_solution(6854731164237918820)
XLA Ops:
  6.5 9.3 %all-to-all-start = ((f32[1,32,104]{2,0,1:T(1,128)}), f32[1,32,104]{2,0,1:T(1,128)S(1)}, u32[]{:S(2)}, u32[]{:S(2)}) async-start(f32[1,32,104]{2,0,1:T(1,128)} %bitcast.154), calls=%async_computation | async-start | bytes 32768 | tf_op jit(solution)/shard_map/all_to_all | solution.py:66
  15.8 1.6 reduce_sum.28
  18.1 1.6 multiply_reduce_fusion
  21.9 71.2 %gather_fusion = f32[13824]{0:T(1024)S(1)} fusion(f32[13824]{0:T(1024)S(1)} %div.38, s32[14336]{0:T(1024)S(1)} %pad_clamp_fusion), kind=kCustom, calls=%fused_computation | custom fusion | bytes 165888 | tf_op jit(solution)/shard_map/gather | solution.py:118
  96.6 1.5 fusion.61
  99.8 1.5 convolution_subtract_fusion.1
  101.5 13.9 %fusion.35 = f32[4,832]{1,0:T(4,128)S(1)} fusion(f32[4,832]{1,0:T(4,128)S(1)} %reshape.51), kind=kOutput, calls=%fused_computation.48 | convolution fusion | flops 39456768 | bytes 26624 | tf_op jit(solution)/shard_map/dot_general | solution.py:44
  115.3 14.1 %fusion.421 = (f32[4]{0:T(128)S(1)}, f32[4,832]{1,0:T(4,128)S(1)}, f32[832,4]{0,1:T(4,128)S(1)}) fusion(f32[4,832]{1,0:T(4,128)S(1)} %fusion.35, f32[4,832]{1,0:T(4,128)S(1)} %reshape.51), kind=kOutput, calls=%fused_computation.402 | convolution fusion | flops 39470076 | bytes 53264 | tf_op jit(solution)/shard_map/dot_general | solution.py:45
  129.7 14.1 %fusion.6 = f32[4,832]{1,0:T(4,128)S(1)} fusion(f32[4,832]{1,0:T(4,128)S(1)} %fusion.35, f32[4,832]{1,0:T(4,128)S(1)} %fusion.186), kind=kOutput, calls=%fused_computation.9 | convolution fusion | flops 39460096 | bytes 39936 | tf_op jit(solution)/shard_map/dot_general | solution.py:52
  143.8 13.7 %fusion.44 = f32[1,4,832]{2,1,0:T(4,128)S(1)} fusion(f32[4,832]{1,0:T(4,128)S(1)} %fusion.6, f32[4,832]{1,0:T(4,128)S(1)} %fusion.186, f32[832,4]{0,1:T(4,128)S(1)} %get-tuple-element.17), kind=kOutput, calls=%fused_computation.51 | convolution fusion | flops 39470080 | bytes 53248 | tf_op jit(solution)/shard_map/dot_general | solution.py:52
  158.8 1.7 reduce.4
  161.3 7.2 %all-to-all-start.1 = ((f32[8,1,416]{2,1,0:T(1,128)}), f32[8,1,416]{2,1,0:T(1,128)S(1)}, u32[]{:S(2)}, u32[]{:S(2)}) async-start(f32[8,1,416]{2,1,0:T(1,128)} %reshape.82), calls=%async_computation.1 | async-start | bytes 32768 | tf_op jit(solution)/shard_map/all_to_all | solution.py:68
  168.6 2.6 fusion.65
  171.2 3.6 all-to-all-done.1
  175.5 1.4 reshape.83
  178.1 1.3 collective-permute-start.1
  179.4 3.0 collective-permute-start
  182.4 2.7 convolution_add_fusion.1
  185.2 3.4 collective-permute-start.3
  188.6 3.9 collective-permute-start.2
  192.6 4.2 collective-permute-done.2
  196.9 71.5 %all_gather.3 = f32[32,56,128]{2,1,0:T(8,128)S(1)} all-gather(f32[1,56,128]{2,1,0:T(8,128)S(1)} %pad_maximum_fusion.1), channel_id=1, replica_groups=mesh['orient'=32,'brow'=2,'bcol'=8] {'orient'}, dimensions={0}, use_global_device_ids=true | all-gather | bytes 946176 | tf_op jit(solution)/shard_map/all_gather | solution.py:89
  274.3 1.5 fusion.55
  277.0 1.5 fusion.59
  278.5 1.5 convolution_subtract_fusion
  280.1 2.3 multiply_subtract_fusion
  285.7 1.2 fusion.53
  288.0 1.2 fusion.49
  289.3 1.2 fusion.32
  293.7 1.8 fusion.34
  295.6 245.6 %all-reduce.2.cloned.1.call-done = f32[32,32,104]{2,1,0:T(8,128)} async-done(((f32[32,32,104]{2,1,0:T(8,128)}), f32[32,32,104]{2,1,0:T(8,128)}) %all-reduce.2.cloned.1.call-update) | async-done | bytes 426000 | tf_op jit(solution)/shard_map/pmax | solution.py:151
  541.2 1.3 constant_dynamic-slice_fusion
  (54 shorter events, 25.5 us)
Async XLA Ops:
  6.5 15.1 %copy-start.2 = (s32[1,13824]{1,0:T(1,128)S(1)}, s32[1,13824]{1,0:T(1,128)}, u32[]{:S(2)}) copy-start(s32[1,13824]{1,0:T(1,128)} %param.5) | copy-start | bytes 165892
  6.5 94.8 %all-to-all-start = ((f32[1,32,104]{2,0,1:T(1,128)}), f32[1,32,104]{2,0,1:T(1,128)S(1)}, u32[]{:S(2)}, u32[]{:S(2)}) async-start(f32[1,32,104]{2,0,1:T(1,128)} %bitcast.154), calls=%async_computation | async-start | bytes 32768 | tf_op jit(solution)/shard_map/all_to_all | solution.py:66
  96.6 1.5 copy-start
  99.0 0.9 copy-start.1
  161.3 13.5 %all-to-all-start.1 = ((f32[8,1,416]{2,1,0:T(1,128)}), f32[8,1,416]{2,1,0:T(1,128)S(1)}, u32[]{:S(2)}, u32[]{:S(2)}) async-start(f32[8,1,416]{2,1,0:T(1,128)} %reshape.82), calls=%async_computation.1 | async-start | bytes 32768 | tf_op jit(solution)/shard_map/all_to_all | solution.py:68
  168.6 372.6 %all-reduce.2.cloned.1.call-start = ((), (), s32[]{:S(2)}) async-start(), calls=%async_computation.2 | async-start | bytes 1048576 | tf_op jit(solution)/shard_map/pmax | solution.py:151
  178.1 7.0 %collective-permute-start.1 = (f32[1,12,104]{2,1,0:T(8,128)S(1)}, f32[1,12,104]{2,1,0:T(8,128)S(1)}, u32[]{:S(2)}, u32[]{:S(2)}) collective-permute-start(f32[1,12,104]{2,1,0:T(8,128)S(1)} %get-tuple-element.12), channel_id=1, source_target_pairs={{8,0},{9,1},{10,2},{11,3},{12,4},{13,5},{14,6},{15,7},{24,16},{25,... | collective-permute-start | bytes 14984 | tf_op jit(solution)/shard_map/ppermute | solution.py:22
  179.4 5.7 %collective-permute-start = (f32[1,12,104]{2,1,0:T(8,128)S(1)}, f32[1,12,104]{2,1,0:T(8,128)S(1)}, u32[]{:S(2)}, u32[]{:S(2)}) collective-permute-start(f32[1,12,104]{2,1,0:T(8,128)S(1)} %get-tuple-element.11), channel_id=1, source_target_pairs={{0,8},{1,9},{2,10},{3,11},{4,12},{5,13},{6,14},{7,15},{16,24},{17,... | collective-permute-start | bytes 14984 | tf_op jit(solution)/shard_map/ppermute | solution.py:20
  185.2 7.4 %collective-permute-start.3 = (f32[1,56,12]{2,1,0:T(8,128)S(1)}, f32[1,56,12]{2,1,0:T(8,128)S(1)}, u32[]{:S(2)}, u32[]{:S(2)}) collective-permute-start(f32[1,56,12]{2,1,0:T(8,128)S(1)} %get-tuple-element.10), channel_id=1, source_target_pairs={{1,0},{2,1},{3,2},{4,3},{5,4},{6,5},{7,6},{9,8},{10,9},{11,10},{12... | collective-permute-start | bytes 8072 | tf_op jit(solution)/shard_map/ppermute | solution.py:22
  188.6 8.2 %collective-permute-start.2 = (f32[1,56,12]{2,1,0:T(8,128)S(1)}, f32[1,56,12]{2,1,0:T(8,128)S(1)}, u32[]{:S(2)}, u32[]{:S(2)}) collective-permute-start(f32[1,56,12]{2,1,0:T(8,128)S(1)} %get-tuple-element.9), channel_id=1, source_target_pairs={{0,1},{1,2},{2,3},{3,4},{4,5},{5,6},{6,7},{8,9},{9,10},{10,11},{11... | collective-permute-start | bytes 8072 | tf_op jit(solution)/shard_map/ppermute | solution.py:20
Sparse Core Ops, SparseCore 0:
  295.7 245.4 all-reduce.1
where the time goes:
time: 558 us; the launch traced here: 550 us
  waiting for transfers between devices  253 us (45%)
  matrix products  95.3 us (17%)
  local copies, waits for them, and re-layouts  78.7 us (14%)
  blocking collectives  71.5 us (13%)
  starting transfers between devices  28.2 us (5%)
  between operations  15.6 us (3%)
  other arithmetic  7.02 us (1%)
    pmax x1, waiting for transfers between devices, shards(): combined = lax.pmax(score, 'orient')  246 us
    all_gather x1, blocking collectives, shards(): portion = lax.all_gather(padded, 'orient', axis=0, tiled=True)  71.5 us
    gather x1, local copies, waits for them, and re-layouts, shards(): normed[voxel_maps[0]].reshape(template_edge, template_edge, template_edge)  71.2 us
    dot_general x1, matrix products, whiten_rows(): jnp.dot(spec_real * weights, cosine, precision=highest)  14.1 us
    dot_general x1, matrix products, whiten_rows(): spec_imag = -jnp.dot(rows_in, sine_table, precision=highest)  14.1 us
    dot_general x1, matrix products, whiten_rows(): spec_real = jnp.dot(rows_in, cosine, precision=highest)  13.9 us
    dot_general x1, matrix products, whiten_rows(): jnp.dot(spec_imag * weights, sine_table, precision=highest)  13.7 us
  transfers between devices with their start and end apart: 7, of which 3 were waited for; matrix products, arithmetic and copies ran while one was open for 16% of the time, Pallas kernels for 0%

commit v1 on v0

--- a/solution.py
+++ b/solution.py
@@ -86,7 +86,10 @@
     box_rows = band_table(out_rows, row_freq, 0, template_edge)
     box_cols = band_table(out_cols, col_freq, 0, template_edge).T
     box_depth = band_table(depth_index, depth_index, -half_edge, half_edge)
-    portion = lax.all_gather(padded, "orient", axis=0, tiled=True)
+    size = lax.axis_size("orient")
+    pieces = jnp.stack([padded for _ in range(size)])
+    pieces = lax.all_to_all(pieces, "orient", split_axis=0, concat_axis=0)
+    portion = jnp.concatenate(pieces, axis=0)
     col_real = jnp.einsum("nxy,yk->nxk", portion, cos_cols, precision=highest)
     col_imag = -jnp.einsum("nxy,yk->nxk", portion, sin_cols, precision=highest)
     spec_real = jnp.einsum("kx,nxy->nky", cos_rows, col_real, precision=highest) + jnp.einsum(

time: 558 us -> 512 us (0.918)
  blocking collectives: 71.5 us -> 25.4 us
  waiting for transfers between devices: 253 us -> 261 us
    all_gather x1 -> x0, blocking collectives: 71.5 us -> none  [shards(): portion = lax.all_gather(padded, 'orient', axis=0, tiled=True)]
    all_to_all x0 -> x2, blocking collectives: none -> 25.4 us  [the longest x1 15.4 us: shards(): lax.all_to_all(volume, 'bcol', split_axis=1, concat_axis=2, tiled=True)]
    pmax x1, waiting for transfers between devices: 246 us -> 256 us  [shards(): combined = lax.pmax(score, 'orient')]
    all_to_all x2 -> x1, starting transfers between devices: 16.5 us -> 14 us  [shards(): pieces = lax.all_to_all(pieces, 'orient', split_axis=0, concat_axis=0)]
  transfers between devices with their start and end apart: 7 -> 6, of which waited for: 3 -> 3; matrix products, arithmetic and copies ran while one was open for 16% -> 17% of each run, Pallas kernels for 0% -> 0%
where the time goes in v1:
time: 512 us; the launch traced here: 503 us
  waiting for transfers between devices  261 us (51%)
  matrix products  94.1 us (18%)
  local copies, waits for them, and re-layouts  76.6 us (15%)
  starting transfers between devices  25.9 us (5%)
  blocking collectives  25.4 us (5%)
  between operations  15.7 us (3%)
    pmax x1, waiting for transfers between devices, shards(): combined = lax.pmax(score, 'orient')  256 us
    gather x1, local copies, waits for them, and re-layouts, shards(): normed[voxel_maps[0]].reshape(template_edge, template_edge, template_edge)  71.3 us
    all_to_all x1, blocking collectives, shards(): lax.all_to_all(volume, 'bcol', split_axis=1, concat_axis=2, tiled=True)  15.4 us
    dot_general x1, matrix products, whiten_rows(): spec_imag = -jnp.dot(rows_in, sine_table, precision=highest)  14.1 us
    all_to_all x1, starting transfers between devices, shards(): pieces = lax.all_to_all(pieces, 'orient', split_axis=0, concat_axis=0)  14 us
    dot_general x1, matrix products, whiten_rows(): spec_real = jnp.dot(rows_in, cosine, precision=highest)  13.9 us
    dot_general x1, matrix products, whiten_rows(): jnp.dot(spec_imag * weights, sine_table, precision=highest)  13.7 us
    dot_general x1, matrix products, whiten_rows(): jnp.dot(spec_real * weights, cosine, precision=highest)  13.6 us
  transfers between devices with their start and end apart: 6, of which 3 were waited for; matrix products, arithmetic and copies ran while one was open for 17% of the time, Pallas kernels for 0%

profile of v1, /device:TPU:2, one launch (start us, length us, event | category | flops | bytes accessed | tf_op | source)
XLA Modules:
  0.0 502.6 jit_solution(7168008265487968231)
XLA Ops:
  6.5 15.4 %all_to_all.38 = f32[1,32,104]{2,0,1:T(1,128)S(1)} all-to-all(f32[1,32,104]{2,0,1:T(1,128)} %bitcast.161), channel_id=1, replica_groups=mesh['orient'=32,'brow'=2,'bcol'=8] {'bcol'}, dimensions={1} | all-to-all | bytes 26624 | tf_op jit(solution)/shard_map/all_to_all | solution.py:66
  22.0 13.9 %fusion.35 = f32[4,832]{1,0:T(4,128)S(1)} fusion(f32[4,832]{1,0:T(4,128)S(1)} %reshape.57), kind=kOutput, calls=%fused_computation.48 | convolution fusion | flops 39456768 | bytes 26624 | tf_op jit(solution)/shard_map/dot_general | solution.py:44
  35.9 14.1 %fusion.422 = (f32[4]{0:T(128)S(1)}, f32[4,832]{1,0:T(4,128)S(1)}, f32[832,4]{0,1:T(4,128)S(1)}) fusion(f32[4,832]{1,0:T(4,128)S(1)} %fusion.35, f32[4,832]{1,0:T(4,128)S(1)} %reshape.57), kind=kOutput, calls=%fused_computation.404 | convolution fusion | flops 39470076 | bytes 53264 | tf_op jit(solution)/shard_map/dot_general | solution.py:45
  50.2 13.6 %fusion.6 = f32[4,832]{1,0:T(4,128)S(1)} fusion(f32[4,832]{1,0:T(4,128)S(1)} %fusion.35, f32[4,832]{1,0:T(4,128)S(1)} %fusion.187), kind=kOutput, calls=%fused_computation.9 | convolution fusion | flops 39460096 | bytes 39936 | tf_op jit(solution)/shard_map/dot_general | solution.py:52
  63.9 13.7 %fusion.44 = f32[1,4,832]{2,1,0:T(4,128)S(1)} fusion(f32[4,832]{1,0:T(4,128)S(1)} %fusion.6, f32[4,832]{1,0:T(4,128)S(1)} %fusion.187, f32[832,4]{0,1:T(4,128)S(1)} %get-tuple-element.17), kind=kOutput, calls=%fused_computation.51 | convolution fusion | flops 39470080 | bytes 53248 | tf_op jit(solution)/shard_map/dot_general | solution.py:52
  78.8 1.7 reduce.4
  80.8 10.1 %all_to_all.39 = f32[8,1,416]{2,1,0:T(1,128)S(1)} all-to-all(f32[8,1,416]{2,1,0:T(1,128)S(1)} %reshape.89), channel_id=1, replica_groups=mesh['orient'=32,'brow'=2,'bcol'=8] {'bcol'}, dimensions={0} | all-to-all | bytes 26624 | tf_op jit(solution)/shard_map/all_to_all | solution.py:68
  92.4 1.4 collective-permute-start.1
  93.8 3.0 collective-permute-start
  97.8 3.4 collective-permute-start.3
  101.2 3.9 collective-permute-start.2
  105.1 4.2 collective-permute-done.2
  110.4 14.0 %all-to-all-start.2 = ((f32[32,1,56,128]{3,2,1,0:T(8,128)}), f32[32,1,56,128]{3,2,1,0:T(8,128)S(1)}, u32[]{:S(2)}, u32[]{:S(2)}) async-start(f32[32,1,56,128]{3,2,1,0:T(8,128)} %stack.2), calls=%async_computation.2 | async-start | bytes 1835008 | tf_op jit(solution)/shard_map/all_to_all | solution.py:91
  127.7 71.3 %gather_fusion = f32[13824]{0:T(1024)S(1)} fusion(f32[13824]{0:T(1024)S(1)} %div.38, s32[14336]{0:T(1024)S(1)} %pad_clamp_fusion), kind=kCustom, calls=%fused_computation | custom fusion | bytes 165888 | tf_op jit(solution)/shard_map/gather | solution.py:121
  203.4 1.5 fusion.63
  205.0 1.5 fusion.67
  206.5 1.6 convolution_subtract_fusion.1
  208.1 2.7 convolution_add_fusion.1
  210.8 1.1 convolution_negate_fusion
  214.1 1.2 fusion.109
  216.4 1.5 fusion.57
  219.0 1.5 fusion.61
  220.5 1.6 convolution_subtract_fusion
  222.2 2.1 multiply_subtract_fusion
  226.4 1.4 convolution_subtract_fusion.2
  227.8 1.2 fusion.55
  230.1 1.2 fusion.51
  231.4 1.2 fusion.32
  233.4 1.2 fusion.31
  236.4 1.9 fusion.34
  238.3 255.6 %all-reduce.2.cloned.1.call-done = f32[32,32,104]{2,1,0:T(8,128)} async-done(((f32[32,32,104]{2,1,0:T(8,128)}), f32[32,32,104]{2,1,0:T(8,128)}) %all-reduce.2.cloned.1.call-update) | async-done | bytes 426000 | tf_op jit(solution)/shard_map/pmax | solution.py:154
  493.9 1.3 constant_dynamic-slice_fusion
  (54 shorter events, 21.4 us)
Async XLA Ops:
  92.4 32.2 %copy-start.1 = (f32[24,24,24]{2,1,0:T(8,128)S(1)}, f32[24,24,24]{2,1,0:T(8,128)}, u32[]{:S(2)}) copy-start(f32[24,24,24]{2,1,0:T(8,128)} %param.4) | copy-start | bytes 165892
  92.4 4.5 collective-permute-start.1
  93.8 3.8 collective-permute-start
  97.8 7.4 %collective-permute-start.3 = (f32[1,56,12]{2,1,0:T(8,128)S(1)}, f32[1,56,12]{2,1,0:T(8,128)S(1)}, u32[]{:S(2)}, u32[]{:S(2)}) collective-permute-start(f32[1,56,12]{2,1,0:T(8,128)S(1)} %get-tuple-element.10), channel_id=1, source_target_pairs={{1,0},{2,1},{3,2},{4,3},{5,4},{6,5},{7,6},{9,8},{10,9},{11,10},{12... | collective-permute-start | bytes 8072 | tf_op jit(solution)/shard_map/ppermute | solution.py:22
  101.2 8.2 %collective-permute-start.2 = (f32[1,56,12]{2,1,0:T(8,128)S(1)}, f32[1,56,12]{2,1,0:T(8,128)S(1)}, u32[]{:S(2)}, u32[]{:S(2)}) collective-permute-start(f32[1,56,12]{2,1,0:T(8,128)S(1)} %get-tuple-element.9), channel_id=1, source_target_pairs={{0,1},{1,2},{2,3},{3,4},{4,5},{5,6},{6,7},{8,9},{9,10},{10,11},{11... | collective-permute-start | bytes 8072 | tf_op jit(solution)/shard_map/ppermute | solution.py:20
  110.4 17.0 %copy-start.2 = (s32[1,13824]{1,0:T(1,128)S(1)}, s32[1,13824]{1,0:T(1,128)}, u32[]{:S(2)}) copy-start(s32[1,13824]{1,0:T(1,128)} %param.5) | copy-start | bytes 165892
  110.4 100.3 %all-to-all-start.2 = ((f32[32,1,56,128]{3,2,1,0:T(8,128)}), f32[32,1,56,128]{3,2,1,0:T(8,128)S(1)}, u32[]{:S(2)}, u32[]{:S(2)}) async-start(f32[32,1,56,128]{3,2,1,0:T(8,128)} %stack.2), calls=%async_computation.2 | async-start | bytes 1835008 | tf_op jit(solution)/shard_map/all_to_all | solution.py:91
  124.5 369.5 %all-reduce.2.cloned.1.call-start = ((), (), s32[]{:S(2)}) async-start(), calls=%async_computation.3 | async-start | bytes 1048576 | tf_op jit(solution)/shard_map/pmax | solution.py:154
  220.5 1.6 copy-start
Sparse Core Ops, SparseCore 0:
  238.4 255.4 all-reduce.1
